TPU v7x, 32 devices: a whole 2x2x4 slice. The times are simulated.
32 devices in a mesh: circ: 2 (over x), len: 4 (over y, core), bank: 4 (over z).
Axes of the slice: x: 2, y: 2, z: 4, core: 2. Of those that a mesh axis runs over, the one named last changes fastest.
Arguments:
- feature_two: bfloat16 [16, 3072, 512], P('circ', ('len', 'bank')), may hold values from -18 to 18
- inner_three: bfloat16 [8, 1536, 512], P('circ', ('len', 'bank')), may hold values from -6 to 6
- skip_three: bfloat16 [8, 1536, 1024], P('circ', ('len', 'bank')), may hold values from -12 to 12
- out_weight: bfloat16 [512, 1024], replicated, may hold values from -0.25 to 0.25
- out_bias: float32 [1024], replicated, may hold values from -3 to 3
- bank_rows: bfloat16 [1280, 1536], P('bank'), may hold values from -6 to 6
- coreset_index: int32 [1024], P('bank'), may hold values from 0 to 319, as said below
Outputs:
- anomaly_map: float32 [16, 3072], P('circ', ('len', 'bank'))
Inputs may be any that keep to these rules, and one draw needn't show every extreme that they name: `coreset_index`: each block of 256 entries names distinct rows among its shard's 320 bank rows.
All inputs are finite; a program needn't handle non-finite values.
Results may differ from a plain program's by a relative error of at most 0.0004.
Values may be sent and summed in bfloat16 or wider, within the bound.
A program may use at most 128 MiB of HBM per device.

v0:
```python
import math

import jax
import jax.numpy as jnp
from jax import lax
from jax.sharding import PartitionSpec as P

RAW_TAPS = [math.exp(-0.5 * (t - 2) * (t - 2)) for t in range(5)]
BLUR_TAPS = [value / sum(RAW_TAPS) for value in RAW_TAPS]


def padded_2(cells, sides, width):
    for axis, dim in sides:
        count = lax.axis_size(axis)
        head = lax.slice_in_dim(cells, 0, width, axis=dim)
        tail = lax.slice_in_dim(cells, cells.shape[dim] - width, cells.shape[dim], axis=dim)
        cells = jnp.concatenate(
            [
                lax.ppermute(tail, axis, [(i, (i + 1) % count) for i in range(count)]),
                cells,
                lax.ppermute(head, axis, [((i + 1) % count, i) for i in range(count)]),
            ],
            axis=dim,
        )
    return cells


def box_mean(extended, height_out, width_out):
    summed = None
    for row_shift in range(3):
        for col_shift in range(3):
            shifted = extended[
                row_shift : row_shift + height_out, col_shift : col_shift + width_out
            ].astype(jnp.float32)
            summed = shifted if summed is None else summed + shifted
    return summed / 9.0


def upsample(padded):
    middle = padded[1:-1]
    upper_rows = 0.75 * middle + 0.25 * padded[:-2]
    lower_rows = 0.75 * middle + 0.25 * padded[2:]
    stretched = jnp.stack([upper_rows, lower_rows], axis=1).reshape(
        -1, padded.shape[1], padded.shape[2]
    )
    center = stretched[:, 1:-1]
    leftside = 0.75 * center + 0.25 * stretched[:, :-2]
    rightside = 0.75 * center + 0.25 * stretched[:, 2:]
    return jnp.stack([leftside, rightside], axis=2).reshape(stretched.shape[0], -1, padded.shape[2])


def nearest(patches, patch_norms, centers, running):
    center_wide = centers.astype(jnp.float32)
    center_norms = jnp.sum(center_wide * center_wide, axis=1)
    products = jnp.dot(patches, centers.T, preferred_element_type=jnp.float32)
    distance = patch_norms[:, None] - 2.0 * products + center_norms[None, :]
    return jnp.minimum(running, jnp.min(distance, axis=1))


def smooth_map(extended, height_out, width_out):
    stretched = None
    for shift in range(5):
        term = BLUR_TAPS[shift] * extended[shift : shift + height_out]
        stretched = term if stretched is None else stretched + term
    result = None
    for shift in range(5):
        term = BLUR_TAPS[shift] * stretched[:, shift : shift + width_out]
        result = term if result is None else result + term
    return result


def open_ends(extended, rim_depth, replicate):
    position = lax.axis_index(("len", "bank"))
    span_count = lax.axis_size(("len", "bank"))
    at_start = position == 0
    at_end = position == span_count - 1
    if replicate:
        leading = jnp.where(at_start, extended[:, 1:2], extended[:, 0:1])
        trailing = jnp.where(at_end, extended[:, -2:-1], extended[:, -1:])
        return jnp.concatenate([leading, extended[:, 1:-1], trailing], axis=1)
    columns = jnp.arange(extended.shape[1], dtype=jnp.int32)
    outside = at_start & (columns < rim_depth) | at_end & (columns >= extended.shape[1] - rim_depth)
    view_shape = (1, extended.shape[1]) + (1,) * (extended.ndim - 2)
    return jnp.where(outside.reshape(view_shape), jnp.zeros((), extended.dtype), extended)


def shards(feature_two, inner_three, skip_three, out_weight, out_bias, bank_rows, coreset_index):
    height_two = feature_two.shape[0]
    width_two = feature_two.shape[1]
    height_three = inner_three.shape[0]
    width_three = inner_three.shape[1]
    rim_two = padded_2(feature_two, (("circ", 0), (("len", "bank"), 1)), 1)
    pooled_two = box_mean(open_ends(rim_two, 1, False), height_two, width_two)
    linear = jnp.dot(
        inner_three.reshape(height_three * width_three, -1),
        out_weight,
        preferred_element_type=jnp.float32,
    )
    linear = linear.reshape(height_three, width_three, -1)
    layer_three = jax.nn.relu(linear + out_bias + skip_three.astype(jnp.float32)).astype(
        jnp.bfloat16
    )
    rim_three = padded_2(layer_three, (("circ", 0), (("len", "bank"), 1)), 2)
    widened_pool = box_mean(
        open_ends(rim_three, 2, False), height_three + 2, width_three + 2
    ).astype(jnp.bfloat16)
    padded_pool = open_ends(widened_pool, 1, True)
    upsampled = upsample(padded_pool.astype(jnp.float32))
    cell_total = height_two * width_two
    patches = (
        jnp.concatenate([pooled_two, upsampled], axis=-1)
        .astype(jnp.bfloat16)
        .reshape(cell_total, -1)
    )
    coreset = jnp.take(bank_rows, coreset_index, axis=0)
    patch_norms = jnp.sum(jnp.square(patches.astype(jnp.float32)), axis=1)
    start_min = jnp.full((cell_total,), jnp.inf, jnp.float32)
    closest = nearest(
        patches, patch_norms, lax.all_gather(coreset, "bank", axis=0, tiled=True), start_min
    )
    scores = (closest / patches.shape[1]).reshape(height_two, width_two)
    rim_scores = padded_2(scores, (("circ", 0), (("len", "bank"), 1)), 2)
    return smooth_map(open_ends(rim_scores, 2, False), height_two, width_two)


def solution(mesh):
    in_specs = (
        P("circ", ("len", "bank"), None),
        P("circ", ("len", "bank"), None),
        P("circ", ("len", "bank"), None),
        P(),
        P(),
        P("bank", None),
        P("bank"),
    )
    out_specs = P("circ", ("len", "bank"))
    return jax.shard_map(shards, mesh=mesh, in_specs=in_specs, out_specs=out_specs, check_vma=False)
```

profile of v0, /device:TPU:0, one launch (start us, length us, event | category | flops | bytes accessed | tf_op | source)
XLA Modules:
  0.0 112.2 jit_solution(18301578795158757602)
XLA Ops:
  6.5 1.9 %fusion.21 = (bf16[1,192,512]{2,1,0:T(8,128)(2,1)}, bf16[1,192,512]{2,1,0:T(8,128)(2,1)}) fusion(bf16[8,192,512]{2,1,0:T(8,128)(2,1)} %param.7), kind=kLoop, calls=%fused_computation.68 | loop fusion | bytes 786432 | tf_op jit(solution)/shard_map/slice | solution.py:15
  8.4 2.9 %collective-permute-start = (bf16[1,192,512]{2,1,0:T(8,128)(2,1)}, bf16[1,192,512]{2,1,0:T(8,128)(2,1)}, u32[]{:S(2)}, u32[]{:S(2)}) collective-permute-start(bf16[1,192,512]{2,1,0:T(8,128)(2,1)} %get-tuple-element.12), channel_id=1, source_target_pairs={{0,16},{16,0},{1,17},{17,1},{2,18},{18,2},{3,19},{19,3},{4,20},{20... | collective-permute-start | bytes 589832 | tf_op jit(solution)/shard_map/ppermute | solution.py:19
  12.7 3.3 %gather_fusion = bf16[256,1536]{1,0:T(8,128)(2,1)S(1)} fusion(bf16[320,1536]{1,0:T(8,128)(2,1)} %param.12, s32[1024]{0:T(1024)S(1)} %pad_clamp_fusion), kind=kCustom, calls=%fused_computation | custom fusion | bytes 1573888 | tf_op jit(solution)/shard_map/jit(_take)/gather | solution.py:115
  17.1 2.0 %maximum_convert_fusion = bf16[4,96,1024]{2,1,0:T(8,128)(2,1)S(1)} fusion(bf16[4,96,1024]{2,1,0:T(8,128)(2,1)} %param.9, bf16[4,96,512]{2,1,0:T(8,128)(2,1)} %param.8, bf16[512,1024]{1,0:T(8,128)(2,1)S(1)} %copy-done, f32[1024]{0:T(1024)S(1)} %copy-done.3), kind=kOutput, calls=%fused_computation.27 | convolution fusion | flops 404619264 | bytes 3018752 | tf_op jit(solution)/shard_map/dot_general | solution.py:94
  20.1 2.0 %collective-permute-start.5 = (bf16[2,96,1024]{2,1,0:T(8,128)(2,1)}, bf16[2,96,1024]{2,1,0:T(8,128)(2,1)}, u32[]{:S(2)}, u32[]{:S(2)}) collective-permute-start(bf16[2,96,1024]{2,1,0:T(8,128)(2,1)} %get-tuple-element.18), channel_id=1, source_target_pairs={{16,0},{0,16},{17,1},{1,17},{18,2},{2,18},{19,3},{3,19},{20,4},{4,... | collective-permute-start | bytes 1179656 | tf_op jit(solution)/shard_map/ppermute | solution.py:21
  23.3 20.3 %collective-permute-done.1 = bf16[1,192,512]{2,1,0:T(8,128)(2,1)} collective-permute-done((bf16[1,192,512]{2,1,0:T(8,128)(2,1)}, bf16[1,192,512]{2,1,0:T(8,128)(2,1)}, u32[]{:S(2)}, u32[]{:S(2)}) %collective-permute-start.1) | collective-permute-done | bytes 196640 | tf_op jit(solution)/shard_map/ppermute | solution.py:21
  44.6 1.6 %collective-permute-start.2 = (bf16[10,1,512]{2,1,0:T(2,128)(2,1)S(1)}, bf16[10,1,512]{2,1,0:T(2,128)(2,1)S(1)}, u32[]{:S(2)}, u32[]{:S(2)}) collective-permute-start(bf16[10,1,512]{2,1,0:T(2,128)(2,1)S(1)} %get-tuple-element.9), channel_id=1, source_target_pairs={{0,1},{1,2},{2,3},{3,4},{4,5},{5,6},{6,7},{7,8},{8,9},{9,10},{10,1... | collective-permute-start | bytes 30728 | tf_op jit(solution)/shard_map/ppermute | solution.py:19
  46.2 2.9 %collective-permute-start.3 = (bf16[10,1,512]{2,1,0:T(2,128)(2,1)S(1)}, bf16[10,1,512]{2,1,0:T(2,128)(2,1)S(1)}, u32[]{:S(2)}, u32[]{:S(2)}) collective-permute-start(bf16[10,1,512]{2,1,0:T(2,128)(2,1)S(1)} %get-tuple-element.10), channel_id=1, source_target_pairs={{1,0},{2,1},{3,2},{4,3},{5,4},{6,5},{7,6},{8,7},{9,8},{10,9},{11,1... | collective-permute-start | bytes 30728 | tf_op jit(solution)/shard_map/ppermute | solution.py:21
  49.1 1.9 %collective-permute-done.2 = bf16[10,1,512]{2,1,0:T(2,128)(2,1)S(1)} collective-permute-done((bf16[10,1,512]{2,1,0:T(2,128)(2,1)S(1)}, bf16[10,1,512]{2,1,0:T(2,128)(2,1)S(1)}, u32[]{:S(2)}, u32[]{:S(2)}) %collective-permute-start.2) | collective-permute-done | bytes 10272 | tf_op jit(solution)/shard_map/ppermute | solution.py:19
  51.1 1.7 %collective-permute-done.3 = bf16[10,1,512]{2,1,0:T(2,128)(2,1)S(1)} collective-permute-done((bf16[10,1,512]{2,1,0:T(2,128)(2,1)S(1)}, bf16[10,1,512]{2,1,0:T(2,128)(2,1)S(1)}, u32[]{:S(2)}, u32[]{:S(2)}) %collective-permute-start.3) | collective-permute-done | bytes 10272 | tf_op jit(solution)/shard_map/ppermute | solution.py:21
  54.5 4.4 %collective-permute-start.7 = (bf16[8,2,1024]{2,1,0:T(2,128)(2,1)S(1)}, bf16[8,2,1024]{2,1,0:T(2,128)(2,1)S(1)}, u32[]{:S(2)}, u32[]{:S(2)}) collective-permute-start(bf16[8,2,1024]{2,1,0:T(2,128)(2,1)S(1)} %get-tuple-element.14), channel_id=1, source_target_pairs={{1,0},{2,1},{3,2},{4,3},{5,4},{6,5},{7,6},{8,7},{9,8},{10,9},{11,1... | collective-permute-start | bytes 98312 | tf_op jit(solution)/shard_map/ppermute | solution.py:21
  58.9 2.5 %multiply_convert_fusion = bf16[8,192,512]{2,1,0:T(8,128)(2,1)S(1)} fusion(bf16[10,194,512]{2,1,0:T(8,128)(2,1)S(1)} %maximum_select_fusion), kind=kLoop, calls=%fused_computation.14 | loop fusion | flops 14942208 | bytes 15728640 | tf_op jit(solution)/shard_map/convert.7
  61.5 1.8 %maximum_select_fusion.1 = bf16[8,100,1024]{2,1,0:T(8,128)(2,1)S(1)} fusion(bf16[8,2,1024]{2,1,0:T(2,128)(2,1)S(1)} %collective-permute-done.7, bf16[2,96,1024]{2,1,0:T(8,128)(2,1)} %collective-permute-done.5, bf16[4,96,1024]{2,1,0:T(8,128)(2,1)S(1)} %maximum_convert_fusion, bf16[2,96,1024]{2,1,0:T(8,128)(2,1)} %collective-permute-done.4, ...), kind=kLoop, calls=%fused_computation.24 | loop fusion | flops 9011200 | bytes 3276900 | tf_op jit(solution)/shard_map/jit(_where)/select_n | solution.py:84
  63.3 2.1 %multiply_convert_fusion.1 = bf16[6,98,1024]{2,1,0:T(8,128)(2,1)S(1)} fusion(bf16[8,100,1024]{2,1,0:T(8,128)(2,1)S(1)} %maximum_select_fusion.1), kind=kLoop, calls=%fused_computation.15 | loop fusion | flops 11440128 | bytes 12042240 | tf_op jit(solution)/shard_map/convert_element_type | solution.py:106
  69.0 5.0 %copy.9 = bf16[8,96,2,1024]{3,2,1,0:T(2,128)(2,1)} copy(bf16[8,96,2,1024]{3,1,0,2:T(8,128)(2,1)S(1)} %pad_maximum_fusion.2) | data formatting | bytes 6291456 | tf_op jit(solution)/shard_map/stack | solution.py:49
  73.9 5.7 %concatenate.36 = bf16[1536,1024]{1,0:T(8,128)(2,1)} reshape(bf16[8,96,2,1024]{3,2,1,0:T(2,128)(2,1)} %copy.9) | data formatting | bytes 6291456 | tf_op jit(solution)/shard_map/concatenate | solution.py:111
  79.7 2.9 %multiply_reduce_fusion = f32[1536]{0:T(1024)S(1)} fusion(bf16[1536,1024]{1,0:T(8,128)(2,1)} %concatenate.36, bf16[1536,512]{1,0:T(8,128)(2,1)S(1)} %bitcast.16), kind=kLoop, calls=%fused_computation.1 | loop fusion | flops 14154240 | bytes 4724736 | tf_op jit(solution)/shard_map/reduce_sum | solution.py:116
  83.3 2.7 %multiply_reduce_fusion.1 = f32[1024]{0:T(1024)S(1)} fusion(bf16[1024,1536]{1,0:T(8,128)(2,1)} %all-gather.2.cloned.1.call-done), kind=kLoop, calls=%fused_computation.3 | loop fusion | flops 4717568 | bytes 3149824 | tf_op jit(solution)/shard_map/reduce_sum | solution.py:54
  86.1 7.3 %add_reduce_fusion = f32[1536]{0:T(1024)S(1)} fusion(bf16[1024,1536]{1,0:T(8,128)(2,1)} %all-gather.2.cloned.1.call-done, f32[1024]{0:T(1024)S(1)} %multiply_reduce_fusion.1, f32[1536]{0:T(1024)S(1)} %multiply_reduce_fusion, bf16[1536,1024]{1,0:T(8,128)(2,1)S(1)} %copy-done.1, bf16[1536,512]{1,0:T(8,128)(2,1)S(1)} %bitcast.17), kind=kOutput, calls=%fused_computation.2 | convolution fusion | flops 4847565312 | bytes 7880704 | tf_op jit(solution)/shard_map/dot_general | solution.py:55
  93.5 1.5 %collective-permute-start.8 = (f32[2,192]{1,0:T(2,128)S(1)}, f32[2,192]{1,0:T(2,128)S(1)}, u32[]{:S(2)}, u32[]{:S(2)}) collective-permute-start(f32[2,192]{1,0:T(2,128)S(1)} %slice.201), channel_id=1, source_target_pairs={{0,16},{16,0},{1,17},{17,1},{2,18},{18,2},{3,19},{19,3},{4,20},{20... | collective-permute-start | bytes 4616 | tf_op jit(solution)/shard_map/ppermute | solution.py:19
  95.7 1.4 %collective-permute-done.8 = f32[2,192]{1,0:T(2,128)S(1)} collective-permute-done((f32[2,192]{1,0:T(2,128)S(1)}, f32[2,192]{1,0:T(2,128)S(1)}, u32[]{:S(2)}, u32[]{:S(2)}) %collective-permute-start.8) | collective-permute-done | bytes 1568 | tf_op jit(solution)/shard_map/ppermute | solution.py:19
  97.1 1.6 %collective-permute-done.9 = f32[2,192]{1,0:T(2,128)S(1)} collective-permute-done((f32[2,192]{1,0:T(2,128)S(1)}, f32[2,192]{1,0:T(2,128)S(1)}, u32[]{:S(2)}, u32[]{:S(2)}) %collective-permute-start.9) | collective-permute-done | bytes 1568 | tf_op jit(solution)/shard_map/ppermute | solution.py:21
  98.8 4.4 %collective-permute-start.11 = (f32[12,2]{1,0:T(8,128)S(1)}, f32[12,2]{1,0:T(8,128)S(1)}, u32[]{:S(2)}, u32[]{:S(2)}) collective-permute-start(f32[12,2]{1,0:T(8,128)S(1)} %get-tuple-element.20), channel_id=1, source_target_pairs={{1,0},{2,1},{3,2},{4,3},{5,4},{6,5},{7,6},{8,7},{9,8},{10,9},{11,1... | collective-permute-start | bytes 296 | tf_op jit(solution)/shard_map/ppermute | solution.py:21
  103.3 1.3 %collective-permute-done.10 = f32[12,2]{1,0:T(8,128)S(1)} collective-permute-done((f32[12,2]{1,0:T(8,128)S(1)}, f32[12,2]{1,0:T(8,128)S(1)}, u32[]{:S(2)}, u32[]{:S(2)}) %collective-permute-start.10) | collective-permute-done | bytes 128 | tf_op jit(solution)/shard_map/ppermute | solution.py:19
  (54 shorter events, 13.3 us)
Async XLA Ops:
  6.5 10.6 %copy-start = (bf16[512,1024]{1,0:T(8,128)(2,1)S(1)}, bf16[512,1024]{1,0:T(8,128)(2,1)}, u32[]{:S(2)}) copy-start(bf16[512,1024]{1,0:T(8,128)(2,1)} %param.10) | copy-start | bytes 3145732
  6.5 76.7 %all-gather.2.cloned.1.call-start = ((), (), s32[]{:S(2)}) async-start(), calls=%async_computation | async-start | bytes 3932160 | tf_op jit(solution)/shard_map/all_gather | solution.py:119
  8.4 13.8 %collective-permute-start = (bf16[1,192,512]{2,1,0:T(8,128)(2,1)}, bf16[1,192,512]{2,1,0:T(8,128)(2,1)}, u32[]{:S(2)}, u32[]{:S(2)}) collective-permute-start(bf16[1,192,512]{2,1,0:T(8,128)(2,1)} %get-tuple-element.12), channel_id=1, source_target_pairs={{0,16},{16,0},{1,17},{17,1},{2,18},{18,2},{3,19},{19,3},{4,20},{20... | collective-permute-start | bytes 589832 | tf_op jit(solution)/shard_map/ppermute | solution.py:19
  12.7 4.4 %copy-start.3 = (f32[1024]{0:T(1024)S(1)}, f32[1024]{0:T(1024)}, u32[]{:S(2)}) copy-start(f32[1024]{0:T(1024)} %param.11) | copy-start | bytes 12292
  17.1 6.0 %copy-start.2 = (bf16[8,192,512]{2,1,0:T(8,128)(2,1)S(1)}, bf16[8,192,512]{2,1,0:T(8,128)(2,1)}, u32[]{:S(2)}) copy-start(bf16[8,192,512]{2,1,0:T(8,128)(2,1)} %param.7) | copy-start | bytes 4718596
  20.1 33.5 %collective-permute-start.4 = (bf16[2,96,1024]{2,1,0:T(8,128)(2,1)}, bf16[2,96,1024]{2,1,0:T(8,128)(2,1)}, u32[]{:S(2)}, u32[]{:S(2)}) collective-permute-start(bf16[2,96,1024]{2,1,0:T(8,128)(2,1)} %get-tuple-element.17), channel_id=1, source_target_pairs={{0,16},{16,0},{1,17},{17,1},{2,18},{18,2},{3,19},{19,3},{4,20},{20... | collective-permute-start | bytes 1179656 | tf_op jit(solution)/shard_map/ppermute | solution.py:19
  20.1 33.5 %collective-permute-start.5 = (bf16[2,96,1024]{2,1,0:T(8,128)(2,1)}, bf16[2,96,1024]{2,1,0:T(8,128)(2,1)}, u32[]{:S(2)}, u32[]{:S(2)}) collective-permute-start(bf16[2,96,1024]{2,1,0:T(8,128)(2,1)} %get-tuple-element.18), channel_id=1, source_target_pairs={{16,0},{0,16},{17,1},{1,17},{18,2},{2,18},{19,3},{3,19},{20,4},{4,... | collective-permute-start | bytes 1179656 | tf_op jit(solution)/shard_map/ppermute | solution.py:21
  22.1 21.5 %collective-permute-start.1 = (bf16[1,192,512]{2,1,0:T(8,128)(2,1)}, bf16[1,192,512]{2,1,0:T(8,128)(2,1)}, u32[]{:S(2)}, u32[]{:S(2)}) collective-permute-start(bf16[1,192,512]{2,1,0:T(8,128)(2,1)} %get-tuple-element.11), channel_id=1, source_target_pairs={{16,0},{0,16},{17,1},{1,17},{18,2},{2,18},{19,3},{3,19},{20,4},{4,... | collective-permute-start | bytes 589832 | tf_op jit(solution)/shard_map/ppermute | solution.py:21
  44.6 6.5 %collective-permute-start.2 = (bf16[10,1,512]{2,1,0:T(2,128)(2,1)S(1)}, bf16[10,1,512]{2,1,0:T(2,128)(2,1)S(1)}, u32[]{:S(2)}, u32[]{:S(2)}) collective-permute-start(bf16[10,1,512]{2,1,0:T(2,128)(2,1)S(1)} %get-tuple-element.9), channel_id=1, source_target_pairs={{0,1},{1,2},{2,3},{3,4},{4,5},{5,6},{6,7},{7,8},{8,9},{9,10},{10,1... | collective-permute-start | bytes 30728 | tf_op jit(solution)/shard_map/ppermute | solution.py:19
  46.2 6.5 %collective-permute-start.3 = (bf16[10,1,512]{2,1,0:T(2,128)(2,1)S(1)}, bf16[10,1,512]{2,1,0:T(2,128)(2,1)S(1)}, u32[]{:S(2)}, u32[]{:S(2)}) collective-permute-start(bf16[10,1,512]{2,1,0:T(2,128)(2,1)S(1)} %get-tuple-element.10), channel_id=1, source_target_pairs={{1,0},{2,1},{3,2},{4,3},{5,4},{6,5},{7,6},{8,7},{9,8},{10,9},{11,1... | collective-permute-start | bytes 30728 | tf_op jit(solution)/shard_map/ppermute | solution.py:21
  54.4 7.1 %collective-permute-start.6 = (bf16[8,2,1024]{2,1,0:T(2,128)(2,1)S(1)}, bf16[8,2,1024]{2,1,0:T(2,128)(2,1)S(1)}, u32[]{:S(2)}, u32[]{:S(2)}) collective-permute-start(bf16[8,2,1024]{2,1,0:T(2,128)(2,1)S(1)} %get-tuple-element.13), channel_id=1, source_target_pairs={{0,1},{1,2},{2,3},{3,4},{4,5},{5,6},{6,7},{7,8},{8,9},{9,10},{10,1... | collective-permute-start | bytes 98312 | tf_op jit(solution)/shard_map/ppermute | solution.py:19
  54.5 7.0 %collective-permute-start.7 = (bf16[8,2,1024]{2,1,0:T(2,128)(2,1)S(1)}, bf16[8,2,1024]{2,1,0:T(2,128)(2,1)S(1)}, u32[]{:S(2)}, u32[]{:S(2)}) collective-permute-start(bf16[8,2,1024]{2,1,0:T(2,128)(2,1)S(1)} %get-tuple-element.14), channel_id=1, source_target_pairs={{1,0},{2,1},{3,2},{4,3},{5,4},{6,5},{7,6},{8,7},{9,8},{10,9},{11,1... | collective-permute-start | bytes 98312 | tf_op jit(solution)/shard_map/ppermute | solution.py:21
  83.3 2.8 %copy-start.1 = (bf16[1536,1024]{1,0:T(8,128)(2,1)S(1)}, bf16[1536,1024]{1,0:T(8,128)(2,1)}, u32[]{:S(2)}) copy-start(bf16[1536,1024]{1,0:T(8,128)(2,1)} %concatenate.36) | copy-start | bytes 9437188
  93.5 3.6 %collective-permute-start.8 = (f32[2,192]{1,0:T(2,128)S(1)}, f32[2,192]{1,0:T(2,128)S(1)}, u32[]{:S(2)}, u32[]{:S(2)}) collective-permute-start(f32[2,192]{1,0:T(2,128)S(1)} %slice.201), channel_id=1, source_target_pairs={{0,16},{16,0},{1,17},{17,1},{2,18},{18,2},{3,19},{19,3},{4,20},{20... | collective-permute-start | bytes 4616 | tf_op jit(solution)/shard_map/ppermute | solution.py:19
  95.1 3.6 %collective-permute-start.9 = (f32[2,192]{1,0:T(2,128)S(1)}, f32[2,192]{1,0:T(2,128)S(1)}, u32[]{:S(2)}, u32[]{:S(2)}) collective-permute-start(f32[2,192]{1,0:T(2,128)S(1)} %slice.203), channel_id=1, source_target_pairs={{16,0},{0,16},{17,1},{1,17},{18,2},{2,18},{19,3},{3,19},{20,4},{4,... | collective-permute-start | bytes 4616 | tf_op jit(solution)/shard_map/ppermute | solution.py:21
  98.8 5.8 %collective-permute-start.10 = (f32[12,2]{1,0:T(8,128)S(1)}, f32[12,2]{1,0:T(8,128)S(1)}, u32[]{:S(2)}, u32[]{:S(2)}) collective-permute-start(f32[12,2]{1,0:T(8,128)S(1)} %get-tuple-element.19), channel_id=1, source_target_pairs={{0,1},{1,2},{2,3},{3,4},{4,5},{5,6},{6,7},{7,8},{8,9},{9,10},{10,1... | collective-permute-start | bytes 296 | tf_op jit(solution)/shard_map/ppermute | solution.py:19
  98.8 5.8 %collective-permute-start.11 = (f32[12,2]{1,0:T(8,128)S(1)}, f32[12,2]{1,0:T(8,128)S(1)}, u32[]{:S(2)}, u32[]{:S(2)}) collective-permute-start(f32[12,2]{1,0:T(8,128)S(1)} %get-tuple-element.20), channel_id=1, source_target_pairs={{1,0},{2,1},{3,2},{4,3},{5,4},{6,5},{7,6},{8,7},{9,8},{10,9},{11,1... | collective-permute-start | bytes 296 | tf_op jit(solution)/shard_map/ppermute | solution.py:21
Sparse Core Ops, SparseCore 0:
  17.2 65.9 all-gather.1
where the time goes:
time: 113 us; the launch traced here: 112 us
  waiting for transfers between devices  29.1 us (26%)
  starting transfers between devices  20.5 us (18%)
  local copies, waits for them, and re-layouts  19.9 us (18%)
  other arithmetic  19.8 us (18%)
  between operations  13.7 us (12%)
  matrix products  9.32 us (8%)
    ppermute x6, waiting for transfers between devices, padded_2(): lax.ppermute(head, axis, [((i + 1) % count, i) for i in range(count)])  23.6 us
    ppermute x6, starting transfers between devices, padded_2(): lax.ppermute(head, axis, [((i + 1) % count, i) for i in range(count)])  14.3 us
    dot_general x1, matrix products, nearest(): products = jnp.dot(patches, centers.T, preferred_element_type=jnp.float32)  7.34 us
    ppermute x6, starting transfers between devices, padded_2(): lax.ppermute(tail, axis, [(i, (i + 1) % count) for i in range(count)])  6.15 us
    concatenate x1, local copies, waits for them, and re-layouts, shards(): jnp.concatenate([pooled_two, upsampled], axis=-1).astype(jnp.bfloat16)  5.72 us
    another operation x1, local copies, waits for them, and re-layouts, upsample(): jnp.stack([leftside, rightside], axis=2)  4.95 us
    ppermute x6, waiting for transfers between devices, padded_2(): lax.ppermute(tail, axis, [(i, (i + 1) % count) for i in range(count)])  4.71 us
    gather x1, local copies, waits for them, and re-layouts, shards(): coreset = jnp.take(bank_rows, coreset_index, axis=0)  3.33 us
  transfers between devices with their start and end apart: 13, of which 7 were waited for; matrix products, arithmetic and copies ran while one was open for 32% of the time, Pallas kernels for 0%

commit v1 on v0

v1 whole, which is shorter than its diff:
```python
import math

import jax
import jax.numpy as jnp
from jax import lax
from jax.experimental import pallas as pl
from jax.experimental.pallas import tpu as pltpu
from jax.sharding import PartitionSpec as P

RAW_TAPS = [math.exp(-0.5 * (t - 2) * (t - 2)) for t in range(5)]
BLUR_TAPS = [value / sum(RAW_TAPS) for value in RAW_TAPS]
MESH = pl.DeviceIdType.MESH
F32 = jnp.float32
BF16 = jnp.bfloat16
VMEM = pltpu.VMEM


def places():
    circ, span, bank = (lax.axis_index(a) for a in ("circ", "len", "bank"))
    n_circ, n_len, n_bank = (lax.axis_size(a) for a in ("circ", "len", "bank"))
    up, down = lax.rem(circ + n_circ - 1, n_circ), lax.rem(circ + 1, n_circ)
    total = n_len * n_bank
    flat = span * n_bank + bank
    before, after = lax.rem(flat + total - 1, total), lax.rem(flat + 1, total)
    left = (before // n_bank, lax.rem(before, n_bank))
    right = (after // n_bank, lax.rem(after, n_bank))
    sides = [(circ,) + left, (circ,) + right]
    corners = [(c,) + s for s in (left, right) for c in (up, down)]
    return (up, span, bank), (down, span, bank), sides, corners, flat == 0, flat == total - 1


def meet(devices):
    barrier = pltpu.get_barrier_semaphore()
    for device in devices:
        pl.semaphore_signal(barrier, inc=1, device_id=device, device_id_type=MESH)
    pl.semaphore_wait(barrier, len(devices))


def travel(own, feature, layer, pack, others, f_up, f_down, l_up, l_down, packs,
           z_send, z_recv, y_send, y_recv, c_send, c_recv, h_send, h_recv):
    circ, span, bank = (lax.axis_index(a) for a in ("circ", "len", "bank"))
    n_len, n_bank = lax.axis_size("len"), lax.axis_size("bank")
    up, down, sides, corners, _, _ = places()
    across = lax.rem(span + 2, n_len)
    mate = (span // 2) * 2 + 1 - lax.rem(span, 2)
    mate_across = lax.rem(mate + 2, n_len)
    z_peers = [(circ, span, lax.rem(bank + d, n_bank)) for d in range(1, n_bank)]
    y_peer, c_peer = (circ, across, bank), (circ, mate, bank)
    meet([up, down] + sides + corners + z_peers + [y_peer, c_peer])
    piece = own.shape[0] // n_len

    def rows(owner):
        return pl.ds(pl.multiple_of(owner * piece, piece), piece)

    def send(src, dst, s, r, device):
        return pltpu.make_async_remote_copy(src, dst, s, r, device_id=device, device_id_type=MESH)

    z = [send(own.at[rows(span)], others.at[d, rows(span)], z_send.at[d], z_recv.at[d], z_peers[d])
         for d in range(n_bank - 1)]
    height = feature.shape[0]
    deep = layer.shape[0]
    halo = [
        (layer.at[deep - 2:deep], l_up, down), (layer.at[0:2], l_down, up),
        (feature.at[height - 1:height], f_up, down), (feature.at[0:1], f_down, up),
        (pack, packs.at[3], sides[0]), (pack, packs.at[0], sides[1]),
        (pack, packs.at[5], corners[0]), (pack, packs.at[4], corners[1]),
        (pack, packs.at[2], corners[2]), (pack, packs.at[1], corners[3]),
    ]
    h = [send(s, d, h_send.at[i], h_recv.at[i], to) for i, (s, d, to) in enumerate(halo)]
    for copy in z:
        copy.start()
    for copy in h:
        copy.start()
    y, c = [], []
    for d in range(n_bank - 1):
        z[d].wait_recv()
        here = others.at[d, rows(span)]
        y.append(send(here, here, y_send.at[d], y_recv.at[d], y_peer))
        y[-1].start()
        c.append(send(here, here, c_send.at[d], c_recv.at[d], c_peer))
        c[-1].start()
    for d in range(n_bank - 1):
        y[d].wait_recv()
        here = others.at[d, rows(across)]
        k = n_bank - 1 + d
        c.append(send(here, here, c_send.at[k], c_recv.at[k], c_peer))
        c[-1].start()
    for copy in c:
        copy.wait_recv()
    for copy in h:
        copy.wait_recv()
    for copy in z + y + c + h:
        copy.wait_send()


def shift_rows(x, by, edge):
    n = x.shape[0]
    moved = pltpu.roll(x, by % n, 0)
    at = 0 if by == 1 else n - 1
    return jnp.where(lax.broadcasted_iota(jnp.int32, x.shape, 0) == at, edge, moved)


def score(feature, layer, f_up, f_down, l_up, l_down, packs, own, others, out, pooled):
    _, _, _, _, at_start, at_end = places()
    height, width, c2 = feature.shape
    deep, wide, c3 = layer.shape
    lead = jnp.where(at_start, 0.0, 1.0)
    trail = jnp.where(at_end, 0.0, 1.0)
    pk = [packs[i].astype(F32) * (lead if i < 3 else trail) for i in range(6)]

    def f_row(r):
        return (f_up[0] if r < 0 else f_down[0] if r >= height else feature[r]).astype(F32)

    def l_row(r):
        return (l_up[r + 2] if r < 0 else l_down[r - deep] if r >= deep else layer[r]).astype(F32)

    def pick(side, r, depth):
        which = side * 3 + (1 if r < 0 else 2 if r >= depth else 0)
        return pk[which], r % depth

    def f_edge(side, r):
        package, row = pick(side, r, height)
        at = row + (8 if side == 0 else 0)
        return package[at:at + 1, :c2]

    def l_edge(side, r, column):
        package, row = pick(side, r, deep)
        at = 2 * row + column + (8 if side == 0 else 0)
        return package[at:at + 1, c2:]

    q_lead, q_trail = [], []
    for k in range(-1, deep + 1):
        s = l_row(k - 1) + l_row(k) + l_row(k + 1)
        e = [[sum(l_edge(side, k + t, column) for t in (-1, 0, 1)) for column in (0, 1)] for side in (0, 1)]
        q = ((s + shift_rows(s, 1, e[0][1]) + shift_rows(s, -1, e[1][0])) / 9.0).astype(BF16)
        pooled[k + 1] = q
        first = ((e[0][0] + e[0][1] + s[0:1]) / 9.0).astype(BF16).astype(F32)
        last = ((s[wide - 1:wide] + e[1][0] + e[1][1]) / 9.0).astype(BF16).astype(F32)
        qf = q.astype(F32)
        q_lead.append(jnp.where(at_start, qf[0:1], first))
        q_trail.append(jnp.where(at_end, qf[wide - 1:wide], last))

    i = lax.broadcasted_iota(jnp.int32, (width, wide), 0)
    j = lax.broadcasted_iota(jnp.int32, (width, wide), 1)
    k = i // 2
    near = k - 1 + 2 * (i % 2)
    stretch = jnp.where(j == k, 0.75, jnp.where(j == near, 0.25, 0.0)).astype(F32)
    main_w = (0.75 * stretch).astype(BF16)
    side_w = (0.25 * stretch).astype(BF16)
    row_id = lax.broadcasted_iota(jnp.int32, (width, c3), 0)
    norms = []
    for part in range(4):
        c = (own[...] if part == 0 else others[part - 1]).astype(F32)
        norms.append(jnp.sum(c * c, axis=1, keepdims=True))
    ones = jnp.ones((8, 128), F32)
    for r in range(height):
        s = f_row(r - 1) + f_row(r) + f_row(r + 1)
        e = [sum(f_edge(side, r + t) for t in (-1, 0, 1)) for side in (0, 1)]
        two = ((s + shift_rows(s, 1, e[0]) + shift_rows(s, -1, e[1])) / 9.0).astype(BF16)
        a = r // 2 + 1
        b = a + (1 if r % 2 else -1)
        u = jnp.dot(main_w, pooled[a], preferred_element_type=F32)
        u = u + jnp.dot(side_w, pooled[b], preferred_element_type=F32)
        begin = 0.25 * (0.75 * q_lead[a] + 0.25 * q_lead[b])
        end = 0.25 * (0.75 * q_trail[a] + 0.25 * q_trail[b])
        u = u + jnp.where(row_id == 0, begin, 0.0) + jnp.where(row_id == width - 1, end, 0.0)
        patch = jnp.concatenate([two, u.astype(BF16)], axis=1)
        wide_patch = patch.astype(F32)
        square = wide_patch * wide_patch
        folded = sum(square[:, t:t + 128] for t in range(0, c2 + c3, 128))
        size = lax.dot_general(ones, folded, (((1,), (1,)), ((), ())),
                               precision=lax.Precision.HIGHEST, preferred_element_type=F32)[0:1]
        best = None
        for part in range(4):
            c = own[...] if part == 0 else others[part - 1]
            product = lax.dot_general(c, patch, (((1,), (1,)), ((), ())), preferred_element_type=F32)
            low = jnp.min(norms[part] - 2.0 * product, axis=0, keepdims=True)
            best = low if best is None else jnp.minimum(best, low)
        out[r:r + 1, :] = (size + best) / (c2 + c3)


def smooth(scores, out, tiles, h_send, h_recv):
    up, down, sides, corners, at_start, at_end = places()
    meet([up, down] + sides + corners)
    plan = [(0, down), (1, up), (5, sides[0]), (2, sides[1]), (7, corners[0]), (6, corners[1]),
            (4, corners[2]), (3, corners[3])]
    copies = [
        pltpu.make_async_remote_copy(scores, tiles.at[slot], h_send.at[slot], h_recv.at[slot],
                                     device_id=to, device_id_type=MESH)
        for slot, to in plan
    ]
    for copy in copies:
        copy.start()
    for copy in copies:
        copy.wait_recv()
    height, width = scores.shape

    def taps(gap):
        found = jnp.zeros(gap.shape, F32)
        for t in range(5):
            found = jnp.where(gap == t - 2, BLUR_TAPS[t], found)
        return found

    def band(shape, offset):
        i = lax.broadcasted_iota(jnp.int32, shape, 0)
        j = lax.broadcasted_iota(jnp.int32, shape, 1)
        return taps(j - i + offset)

    def dot(a, b):
        return jnp.dot(a, b, precision=lax.Precision.HIGHEST, preferred_element_type=F32)

    vertical = band((height, 3 * height), -height)
    middle = dot(vertical, jnp.concatenate([tiles[0], scores[...], tiles[1]], axis=0))
    left = dot(vertical, jnp.concatenate([tiles[3], tiles[2], tiles[4]], axis=0))
    right = dot(vertical, jnp.concatenate([tiles[6], tiles[5], tiles[7]], axis=0))
    left = left * jnp.where(at_start, 0.0, 1.0)
    right = right * jnp.where(at_end, 0.0, 1.0)
    square = (width, width)
    out[...] = dot(middle, band(square, 0)) + dot(left, band(square, width)) + dot(right, band(square, -width))
    for copy in copies:
        copy.wait_send()


def shards(feature_two, inner_three, skip_three, out_weight, out_bias, bank_rows, coreset_index):
    height, width, c2 = feature_two.shape
    deep, wide, c3 = skip_three.shape
    n_bank = lax.axis_size("bank")
    pick = (coreset_index[:, None] == jnp.arange(bank_rows.shape[0], dtype=jnp.int32)[None, :]).astype(BF16)
    own = jnp.dot(pick, bank_rows, preferred_element_type=F32).astype(BF16)
    linear = jnp.dot(inner_three.reshape(deep * wide, -1), out_weight, preferred_element_type=F32)
    layer = jax.nn.relu(linear.reshape(deep, wide, -1) + out_bias + skip_three.astype(F32)).astype(BF16)
    pack = jnp.concatenate(
        [
            jnp.concatenate([feature_two[:, 0], feature_two[:, width - 1]], axis=0),
            jnp.concatenate(
                [layer[:, :2].reshape(2 * deep, c3), layer[:, wide - 2:].reshape(2 * deep, c3)], axis=0
            ),
        ],
        axis=1,
    )
    vm = pl.BlockSpec(memory_space=VMEM)
    dma = pltpu.SemaphoreType.DMA
    cores = own.shape[0]
    shape = jax.ShapeDtypeStruct
    others, f_up, f_down, l_up, l_down, packs = pl.pallas_call(
        travel,
        out_shape=[
            shape((n_bank - 1, cores, c2 + c3), BF16),
            shape((1, width, c2), BF16), shape((1, width, c2), BF16),
            shape((2, wide, c3), BF16), shape((2, wide, c3), BF16),
            shape((6,) + pack.shape, BF16),
        ],
        in_specs=[vm] * 4,
        out_specs=[vm] * 6,
        scratch_shapes=[dma((n_bank - 1,))] * 4 + [dma((2 * (n_bank - 1),))] * 2 + [dma((10,))] * 2,
        compiler_params=pltpu.CompilerParams(
            collective_id=0, has_side_effects=True, vmem_limit_bytes=40 * 2**20),
    )(own, feature_two, layer, pack)
    scores = pl.pallas_call(
        score,
        out_shape=shape((height, width), F32),
        in_specs=[vm] * 9,
        out_specs=vm,
        scratch_shapes=[VMEM((deep + 2, wide, c3), BF16)],
        compiler_params=pltpu.CompilerParams(vmem_limit_bytes=48 * 2**20),
    )(feature_two, layer, f_up, f_down, l_up, l_down, packs, own, others)
    return pl.pallas_call(
        smooth,
        out_shape=shape((height, width), F32),
        in_specs=[vm],
        out_specs=vm,
        scratch_shapes=[VMEM((8, height, width), F32), dma((8,)), dma((8,))],
        compiler_params=pltpu.CompilerParams(collective_id=1, has_side_effects=True),
    )(scores)


def solution(mesh):
    in_specs = (
        P("circ", ("len", "bank"), None),
        P("circ", ("len", "bank"), None),
        P("circ", ("len", "bank"), None),
        P(),
        P(),
        P("bank", None),
        P("bank"),
    )
    out_specs = P("circ", ("len", "bank"))
    return jax.shard_map(shards, mesh=mesh, in_specs=in_specs, out_specs=out_specs, check_vma=False)
```

time: 113 us -> 68.6 us (0.61)
  Pallas kernels: 0 us -> 59.7 us
  waiting for transfers between devices: 29.1 us -> 0 us
  starting transfers between devices: 20.5 us -> 0 us
  other arithmetic: 19.8 us -> 0.01 us
  local copies, waits for them, and re-layouts: 19.9 us -> 4.65 us
  between operations: 13.7 us -> 0.11 us
  matrix products: 9.32 us -> 3.77 us
    pallas_call x0 -> x3, Pallas kernels: none -> 59.7 us  [the longest x1 37.5 us: shards(): pl.pallas_call(travel, out_shape=[shape((n_bank - 1, cores, c2 + c3), BF1...]
    ppermute x12 -> x0, waiting for transfers between devices: 28.3 us -> none  [the longest x6 23.6 us: padded_2(): lax.ppermute(head, axis, [((i + 1) % count, i) for i in range(count)])]
    ppermute x12 -> x0, starting transfers between devices: 20.5 us -> none  [the longest x6 14.3 us: padded_2(): lax.ppermute(head, axis, [((i + 1) % count, i) for i in range(count)])]
    concatenate x2 -> x0, local copies, waits for them, and re-layouts: 6.66 us -> none  [the longest x1 5.72 us: shards(): jnp.concatenate([pooled_two, upsampled], axis=-1).astype(jnp.bfloat16)]
    reduce_sum x2 -> x0, other arithmetic: 5.59 us -> none  [the longest x1 2.88 us: shards(): patch_norms = jnp.sum(jnp.square(patches.astype(jnp.float32)), axis=1)]
    dot_general x2, matrix products: 9.32 us -> 3.77 us  [the longest x1 1.92 us: shards(): own = jnp.dot(pick, bank_rows, preferred_element_type=F32).astype(BF16)]
    another operation x2 -> x0, local copies, waits for them, and re-layouts: 5.19 us -> none  [the longest x1 4.95 us: upsample(): jnp.stack([leftside, rightside], axis=2)]
    another operation x5 -> x0, other arithmetic: 5.06 us -> none
  transfers between devices with their start and end apart: 13 -> 0, of which waited for: 7 -> 0; matrix products, arithmetic and copies ran while one was open for 32% -> 0% of each run, Pallas kernels for 0% -> 0%
where the time goes in v1:
time: 68.6 us; the launch traced here: 68.3 us
  Pallas kernels  59.7 us (87%)
  local copies, waits for them, and re-layouts  4.65 us (7%)
  matrix products  3.77 us (5%)
    pallas_call x1, Pallas kernels, shards(): pl.pallas_call(travel, out_shape=[shape((n_bank - 1, cores, c2 + c3), BF1...  37.5 us
    pallas_call x1, Pallas kernels, shards(): pl.pallas_call(score, out_shape=shape((height, width), F32), in_specs=[vm...  12.9 us
    pallas_call x1, Pallas kernels, shards(): pl.pallas_call(smooth, out_shape=shape((height, width), F32), in_specs=[v...  9.3 us
    unnamed x11, local copies, waits for them, and re-layouts  3.59 us
    dot_general x1, matrix products, shards(): own = jnp.dot(pick, bank_rows, preferred_element_type=F32).astype(BF16)  1.92 us
    dot_general x1, matrix products, shards(): jnp.dot(inner_three.reshape(deep * wide, -1), out_weight, preferred_eleme...  1.86 us

profile of v1, /device:TPU:0, one launch (start us, length us, event | category | flops | bytes accessed | tf_op | source)
XLA Modules:
  0.0 68.3 jit_solution(3733166467409949388)
XLA Ops:
  0.0 0.0 copy-start
  0.0 1.0 %fusion.2 = (bf16[8,1,512]{2,1,0:T(2,128)(2,1)S(1)}, bf16[8,1,512]{2,1,0:T(2,128)(2,1)S(1)}) fusion(bf16[8,192,512]{2,1,0:T(8,128)(2,1)} %feature.3), kind=kLoop, calls=%fused_computation.8 | loop fusion | bytes 32768 | tf_op jit(solution)/shard_map/slice | solution.py:234
  1.0 0.3 copy-done
  1.3 0.0 copy-start.4
  1.3 1.9 %maximum_convert_fusion.layer = bf16[4,96,1024]{2,1,0:T(8,128)(2,1)S(1)} fusion(bf16[4,96,1024]{2,1,0:T(8,128)(2,1)} %param.9, bf16[4,96,512]{2,1,0:T(8,128)(2,1)} %param.8, bf16[512,1024]{1,0:T(8,128)(2,1)S(1)} %copy-done, f32[1024]{0:T(1024)} %param.11), kind=kOutput, calls=%fused_computation.1 | convolution fusion | flops 404619264 | bytes 3018752 | tf_op jit(solution)/shard_map/dot_general | solution.py:230
  3.2 0.0 copy-start.1
  3.3 0.0 copy-done.4
  3.3 1.9 %convolution_convert_fusion.own = bf16[256,1536]{1,0:T(8,128)(2,1)S(1)} fusion(bf16[320,1536]{1,0:T(8,128)(2,1)} %param.12, s32[256]{0:T(256)S(1)} %copy-done.4), kind=kOutput, calls=%fused_computation | convolution fusion | flops 252133376 | bytes 1770496 | tf_op jit(solution)/shard_map/dot_general | solution.py:229
  5.2 0.0 copy-done.1
  5.2 37.5 %shard_map.73 = (bf16[3,256,1536]{2,1,0:T(8,128)(2,1)S(1)}, bf16[1,192,512]{2,1,0:T(8,128)(2,1)S(1)}, bf16[1,192,512]{2,1,0:T(8,128)(2,1)S(1)}, bf16[2,96,1024]{...) custom-call(bf16[256,1536]{1,0:T(8,128)(2,1)S(1)} %convolution_convert_fusion.own, ...), custom_call_target="tpu_custom_call" | custom-call | tf_op jit(solution)/shard_map/pallas_call | solution.py:245
  42.8 0.0 copy-start.2
  42.8 1.4 %copy-done.2 = bf16[3,256,1536]{2,1,0:T(8,128)(2,1)} copy-done((bf16[3,256,1536]{2,1,0:T(8,128)(2,1)}, bf16[3,256,1536]{2,1,0:T(8,128)(2,1)S(1)}, u32[]{:S(2)}) %copy-start.2) | copy-done | bytes 2359320
  44.2 12.9 %shard_map.74.scores = f32[8,192]{1,0:T(8,128)S(1)} custom-call(bf16[8,192,512]{2,1,0:T(8,128)(2,1)S(1)} %copy-done.1, bf16[4,96,1024]{2,1,0:T(8,128)(2,1)S(1)} %maximum_convert_fusion.layer, bf16[1,192,512]{2,1,0:T(8,128)(2,1)S(1)} %get-tuple-element.11.f_up, bf16[1,192,512]{2,1,0:T(8,128)(2,1)S(1)} %get-tuple-element.12.f_down, ...), custom_call_target="tpu_custom_call" | custom-call | tf_op jit(solution)/shard_map/pallas_call | solution.py:259
  57.1 0.0 copy-start.3
  57.1 0.6 copy-done.3
  57.7 9.3 %shard_map.75 = f32[8,192]{1,0:T(8,128)} custom-call(f32[8,192]{1,0:T(8,128)} %copy-done.3), custom_call_target="tpu_custom_call" | custom-call | tf_op jit(solution)/shard_map/pallas_call | solution.py:267
  67.0 1.3 %copy.15 = f32[8,192]{1,0:T(8,128)} copy(f32[8,192]{1,0:T(8,128)} %shard_map.75) | data formatting | bytes 12288
  (5 shorter events, 0.1 us)
Async XLA Ops:
  0.0 1.3 %copy-start = (bf16[512,1024]{1,0:T(8,128)(2,1)S(1)}, bf16[512,1024]{1,0:T(8,128)(2,1)}, u32[]{:S(2)}) copy-start(bf16[512,1024]{1,0:T(8,128)(2,1)} %param.10) | copy-start | bytes 3145732
  1.3 2.0 %copy-start.4 = (s32[256]{0:T(256)S(1)}, s32[256]{0:T(256)}, u32[]{:S(2)}) copy-start(s32[256]{0:T(256)} %param.13) | copy-start | bytes 3076
  3.2 2.0 %copy-start.1 = (bf16[8,192,512]{2,1,0:T(8,128)(2,1)S(1)}, bf16[8,192,512]{2,1,0:T(8,128)(2,1)}, u32[]{:S(2)}) copy-start(bf16[8,192,512]{2,1,0:T(8,128)(2,1)} %feature.3) | copy-start | bytes 4718596
  42.8 1.4 %copy-start.2 = (bf16[3,256,1536]{2,1,0:T(8,128)(2,1)}, bf16[3,256,1536]{2,1,0:T(8,128)(2,1)S(1)}, u32[]{:S(2)}) copy-start(bf16[3,256,1536]{2,1,0:T(8,128)(2,1)S(1)} %get-tuple-element.16.others) | copy-start | bytes 7077892
  57.1 0.6 copy-start.3

commit v2 on v1

v2 whole, which is shorter than its diff:
```python
import math

import jax
import jax.numpy as jnp
from jax import lax
from jax.experimental import pallas as pl
from jax.experimental.pallas import tpu as pltpu
from jax.sharding import PartitionSpec as P

RAW_TAPS = [math.exp(-0.5 * (t - 2) * (t - 2)) for t in range(5)]
BLUR_TAPS = [value / sum(RAW_TAPS) for value in RAW_TAPS]
MESH = pl.DeviceIdType.MESH
F32 = jnp.float32
BF16 = jnp.bfloat16
VMEM = pltpu.VMEM


def places():
    circ, span, bank = (lax.axis_index(a) for a in ("circ", "len", "bank"))
    n_circ, n_len, n_bank = (lax.axis_size(a) for a in ("circ", "len", "bank"))
    up, down = lax.rem(circ + n_circ - 1, n_circ), lax.rem(circ + 1, n_circ)
    total = n_len * n_bank
    flat = span * n_bank + bank
    before, after = lax.rem(flat + total - 1, total), lax.rem(flat + 1, total)
    left = (before // n_bank, lax.rem(before, n_bank))
    right = (after // n_bank, lax.rem(after, n_bank))
    sides = [(circ,) + left, (circ,) + right]
    corners = [(c,) + s for s in (left, right) for c in (up, down)]
    return (up, span, bank), (down, span, bank), sides, corners, flat == 0, flat == total - 1


def meet(devices):
    barrier = pltpu.get_barrier_semaphore()
    for device in devices:
        pl.semaphore_signal(barrier, inc=1, device_id=device, device_id_type=MESH)
    pl.semaphore_wait(barrier, len(devices))


def shift_rows(x, by, edge):
    n = x.shape[0]
    moved = pltpu.roll(x, by % n, 0)
    at = 0 if by == 1 else n - 1
    return jnp.where(lax.broadcasted_iota(jnp.int32, x.shape, 0) == at, edge, moved)


def send(src, dst, s, r, device):
    return pltpu.make_async_remote_copy(src, dst, s, r, device_id=device, device_id_type=MESH)


def roll_map(feature, inner, skip, weight, bias, bank_rows, index, out,
             layer, pack, cores, f_halo, l_halo, packs, pooled, patches, sizes, bests, scores, tiles,
             z_send, z_recv, y_send, y_recv, c_send, c_recv, h_send, h_recv, t_send, t_recv):
    circ, span, bank = (lax.axis_index(a) for a in ("circ", "len", "bank"))
    n_len, n_bank = lax.axis_size("len"), lax.axis_size("bank")
    up, down, sides, corners, at_start, at_end = places()
    across = lax.rem(span + 2, n_len)
    mate = (span // 2) * 2 + 1 - lax.rem(span, 2)
    z_peers = [(circ, span, lax.rem(bank + d, n_bank)) for d in range(1, n_bank)]
    y_peer, c_peer = (circ, across, bank), (circ, mate, bank)
    meet([up, down] + sides + corners + z_peers + [y_peer, c_peer])
    height, width, c2 = feature.shape
    deep, wide, c3 = skip.shape
    piece = cores.shape[1] // n_len

    def rows(owner):
        return pl.ds(pl.multiple_of(owner * piece, piece), piece)

    halo = [
        (layer.at[deep - 1], l_halo.at[1], down), (layer.at[0], l_halo.at[2], up),
        (feature.at[height - 1], f_halo.at[0], down), (feature.at[0], f_halo.at[1], up),
        (layer.at[deep - 2], l_halo.at[0], down), (layer.at[1], l_halo.at[3], up),
        (pack, packs.at[3], sides[0]), (pack, packs.at[0], sides[1]),
        (pack, packs.at[5], corners[0]), (pack, packs.at[4], corners[1]),
        (pack, packs.at[2], corners[2]), (pack, packs.at[1], corners[3]),
    ]
    h = [send(s, d, h_send.at[i], h_recv.at[i], to) for i, (s, d, to) in enumerate(halo)]

    sixteen = lax.broadcasted_iota(jnp.int32, (16, c3), 0)
    packed = jnp.zeros((16, c3), F32)
    for r in [deep - 1, 0] + list(range(1, deep - 1)):
        linear = jnp.dot(inner[r], weight[...], preferred_element_type=F32)
        value = jnp.maximum(linear + bias[...] + skip[r].astype(F32), 0.0).astype(BF16)
        layer[r] = value
        value = value.astype(F32)
        for column in (0, 1):
            packed = jnp.where(sixteen == 2 * r + column, value[column:column + 1], packed)
            at = wide - 2 + column
            packed = jnp.where(sixteen == 8 + 2 * r + column, value[at:at + 1], packed)
        if r == deep - 1:
            h[0].start()
        if r == 0:
            h[1].start()
            h[2].start()
            h[3].start()
    pack[:, c2:] = packed.astype(BF16)
    sixteen = lax.broadcasted_iota(jnp.int32, (16, c2), 0)
    packed = jnp.zeros((16, c2), F32)
    for r in range(height):
        packed = jnp.where(sixteen == r, feature[r, 0:16].astype(F32)[0:1], packed)
        packed = jnp.where(sixteen == 8 + r, feature[r, width - 16:width].astype(F32)[15:16], packed)
    pack[:, :c2] = packed.astype(BF16)
    for copy in h[6:]:
        copy.start()

    chosen = index[...] == lax.broadcasted_iota(jnp.int32, (cores.shape[1], bank_rows.shape[0]), 1)
    cores[0] = jnp.dot(jnp.where(chosen, 1.0, 0.0).astype(BF16), bank_rows[...],
                       preferred_element_type=F32).astype(BF16)
    z = [send(cores.at[0, rows(span)], cores.at[d + 1, rows(span)], z_send.at[d], z_recv.at[d], z_peers[d])
         for d in range(n_bank - 1)]
    for copy in z:
        copy.start()

    lead = jnp.where(at_start, 0.0, 1.0)
    trail = jnp.where(at_end, 0.0, 1.0)
    for copy in h[6:]:
        copy.wait_recv()
    pk = [packs[i].astype(F32) * (lead if i < 3 else trail) for i in range(6)]

    def f_row(r):
        return (f_halo[0] if r < 0 else f_halo[1] if r >= height else feature[r]).astype(F32)

    def l_row(r):
        return (l_halo[r + 2] if r < 0 else l_halo[2 + r - deep] if r >= deep else layer[r]).astype(F32)

    def pick(side, r, depth):
        which = side * 3 + (1 if r < 0 else 2 if r >= depth else 0)
        return pk[which], r % depth

    def f_edge(side, r):
        package, row = pick(side, r, height)
        at = row + (8 if side == 0 else 0)
        return package[at:at + 1, :c2]

    def l_edge(side, r, column):
        package, row = pick(side, r, deep)
        at = 2 * row + column + (8 if side == 0 else 0)
        return package[at:at + 1, c2:]

    q_lead, q_trail = {}, {}

    def pool_three(k):
        s = l_row(k - 1) + l_row(k) + l_row(k + 1)
        e = [[sum(l_edge(side, k + t, column) for t in (-1, 0, 1)) for column in (0, 1)] for side in (0, 1)]
        q = ((s + shift_rows(s, 1, e[0][1]) + shift_rows(s, -1, e[1][0])) / 9.0).astype(BF16)
        pooled[k + 1] = q
        first = ((e[0][0] + e[0][1] + s[0:1]) / 9.0).astype(BF16).astype(F32)
        last = ((s[wide - 1:wide] + e[1][0] + e[1][1]) / 9.0).astype(BF16).astype(F32)
        qf = q.astype(F32)
        q_lead[k + 1] = jnp.where(at_start, qf[0:1], first)
        q_trail[k + 1] = jnp.where(at_end, qf[wide - 1:wide], last)

    i = lax.broadcasted_iota(jnp.int32, (width, wide), 0)
    j = lax.broadcasted_iota(jnp.int32, (width, wide), 1)
    k = i // 2
    near = k - 1 + 2 * (i % 2)
    stretch = jnp.where(j == k, 0.75, jnp.where(j == near, 0.25, 0.0)).astype(F32)
    main_w = (0.75 * stretch).astype(BF16)
    side_w = (0.25 * stretch).astype(BF16)
    row_id = lax.broadcasted_iota(jnp.int32, (width, c3), 0)
    ones = jnp.ones((8, 128), F32)

    def make_patch(r):
        s = f_row(r - 1) + f_row(r) + f_row(r + 1)
        e = [sum(f_edge(side, r + t) for t in (-1, 0, 1)) for side in (0, 1)]
        two = ((s + shift_rows(s, 1, e[0]) + shift_rows(s, -1, e[1])) / 9.0).astype(BF16)
        a = r // 2 + 1
        b = a + (1 if r % 2 else -1)
        u = jnp.dot(main_w, pooled[a], preferred_element_type=F32)
        u = u + jnp.dot(side_w, pooled[b], preferred_element_type=F32)
        begin = 0.25 * (0.75 * q_lead[a] + 0.25 * q_lead[b])
        end = 0.25 * (0.75 * q_trail[a] + 0.25 * q_trail[b])
        u = u + jnp.where(row_id == 0, begin, 0.0) + jnp.where(row_id == width - 1, end, 0.0)
        patch = jnp.concatenate([two, u.astype(BF16)], axis=1)
        patches[r] = patch
        wide_patch = patch.astype(F32)
        square = wide_patch * wide_patch
        folded = sum(square[:, t:t + 128] for t in range(0, c2 + c3, 128))
        sizes[r] = lax.dot_general(ones, folded, (((1,), (1,)), ((), ())),
                                   precision=lax.Precision.HIGHEST, preferred_element_type=F32)

    for k in range(1, deep - 1):
        pool_three(k)
    for r in range(3, height - 3):
        make_patch(r)
    y, c = [], []
    for d in range(n_bank - 1):
        z[d].wait_recv()
        here = cores.at[d + 1, rows(span)]
        y.append(send(here, here, y_send.at[d], y_recv.at[d], y_peer))
        y[-1].start()
        c.append(send(here, here, c_send.at[d], c_recv.at[d], c_peer))
        c[-1].start()
    h[4].start()
    h[5].start()
    h[0].wait_recv()
    h[1].wait_recv()
    pool_three(0)
    pool_three(deep - 1)
    for r in [1, 2, height - 3, height - 2]:
        make_patch(r)
    for d in range(n_bank - 1):
        y[d].wait_recv()
        here = cores.at[d + 1, rows(across)]
        e = n_bank - 1 + d
        c.append(send(here, here, c_send.at[e], c_recv.at[e], c_peer))
        c[-1].start()
    for copy in c:
        copy.wait_recv()

    norms = []
    for part in range(n_bank):
        wide_core = cores[part].astype(F32)
        norms.append(jnp.sum(wide_core * wide_core, axis=1, keepdims=True))

    def score_row(r, carry):
        patch = patches[r]
        best = None
        for part in range(n_bank):
            product = lax.dot_general(cores[part], patch, (((1,), (1,)), ((), ())), preferred_element_type=F32)
            low = jnp.min(norms[part] - 2.0 * product, axis=0, keepdims=True)
            best = low if best is None else jnp.minimum(best, low)
        bests[r] = jnp.broadcast_to(best, bests.shape[1:])
        return carry

    lax.fori_loop(1, height - 1, score_row, 0)
    for copy in h[2:6]:
        copy.wait_recv()
    pool_three(-1)
    pool_three(deep)
    make_patch(0)
    make_patch(height - 1)
    lax.fori_loop(0, 2, lambda n, carry: score_row(n * (height - 1), carry), 0)

    eight = lax.broadcasted_iota(jnp.int32, (height, width), 0)
    found = jnp.zeros((height, width), F32)
    for r in range(height):
        found = jnp.where(eight == r, (sizes[r][0:1] + bests[r][0:1]) / (c2 + c3), found)
    scores[...] = found
    plan = [(0, down), (1, up), (5, sides[0]), (2, sides[1]), (7, corners[0]), (6, corners[1]),
            (4, corners[2]), (3, corners[3])]
    t = [send(scores, tiles.at[slot], t_send.at[slot], t_recv.at[slot], to) for slot, to in plan]
    for copy in t:
        copy.start()

    def taps(gap):
        weights = jnp.zeros(gap.shape, F32)
        for n in range(5):
            weights = jnp.where(gap == n - 2, BLUR_TAPS[n], weights)
        return weights

    def band(shape, offset):
        i = lax.broadcasted_iota(jnp.int32, shape, 0)
        j = lax.broadcasted_iota(jnp.int32, shape, 1)
        return taps(j - i + offset)

    def dot(a, b):
        return jnp.dot(a, b, precision=lax.Precision.HIGHEST, preferred_element_type=F32)

    vertical = band((height, 3 * height), -height)
    bands = [band((width, width), offset) for offset in (0, width, -width)]
    for copy in z + y + c + h:
        copy.wait_send()
    for copy in t:
        copy.wait_recv()
    middle = dot(vertical, jnp.concatenate([tiles[0], found, tiles[1]], axis=0))
    left = dot(vertical, jnp.concatenate([tiles[3], tiles[2], tiles[4]], axis=0)) * lead
    right = dot(vertical, jnp.concatenate([tiles[6], tiles[5], tiles[7]], axis=0)) * trail
    out[...] = dot(middle, bands[0]) + dot(left, bands[1]) + dot(right, bands[2])
    for copy in t:
        copy.wait_send()


def shards(feature_two, inner_three, skip_three, out_weight, out_bias, bank_rows, coreset_index):
    height, width, c2 = feature_two.shape
    deep, wide, c3 = skip_three.shape
    n_bank = lax.axis_size("bank")
    cores = coreset_index.shape[0]
    vm = pl.BlockSpec(memory_space=VMEM)
    dma = pltpu.SemaphoreType.DMA
    return pl.pallas_call(
        roll_map,
        out_shape=jax.ShapeDtypeStruct((height, width), F32),
        in_specs=[vm] * 7,
        out_specs=vm,
        scratch_shapes=[
            VMEM((deep, wide, c3), BF16),
            VMEM((16, c2 + c3), BF16),
            VMEM((n_bank, cores, c2 + c3), BF16),
            VMEM((2, width, c2), BF16),
            VMEM((4, wide, c3), BF16),
            VMEM((6, 16, c2 + c3), BF16),
            VMEM((deep + 2, wide, c3), BF16),
            VMEM((height, width, c2 + c3), BF16),
            VMEM((height, 8, width), F32),
            VMEM((height, 8, width), F32),
            VMEM((height, width), F32),
            VMEM((8, height, width), F32),
        ] + [dma((n_bank - 1,))] * 4 + [dma((2 * (n_bank - 1),))] * 2 + [dma((12,))] * 2 + [dma((8,))] * 2,
        compiler_params=pltpu.CompilerParams(
            collective_id=0, has_side_effects=True, vmem_limit_bytes=48 * 2**20),
    )(feature_two, inner_three, skip_three, out_weight, out_bias[None, :], bank_rows, coreset_index[:, None])


def solution(mesh):
    in_specs = (
        P("circ", ("len", "bank"), None),
        P("circ", ("len", "bank"), None),
        P("circ", ("len", "bank"), None),
        P(),
        P(),
        P("bank", None),
        P("bank"),
    )
    out_specs = P("circ", ("len", "bank"))
    return jax.shard_map(shards, mesh=mesh, in_specs=in_specs, out_specs=out_specs, check_vma=False)
```

time: 68.6 us -> 65.8 us (0.959)
  matrix products: 3.77 us -> 0 us
  local copies, waits for them, and re-layouts: 4.65 us -> 8.05 us
  Pallas kernels: 59.7 us -> 57.4 us
    dot_general x2 -> x0, matrix products: 3.77 us -> none  [the longest x1 1.92 us: shards(): own = jnp.dot(pick, bank_rows, preferred_element_type=F32).astype(BF16)]
    unnamed x11 -> x13, local copies, waits for them, and re-layouts: 3.59 us -> 7.25 us
    pallas_call x3 -> x1, Pallas kernels: 59.7 us -> 57.4 us  [shards(): pl.pallas_call(roll_map, out_shape=jax.ShapeDtypeStruct((height, width),...]
    slice x2 -> x0, local copies, waits for them, and re-layouts: 1.02 us -> none  [the longest x1 0.99 us: shards(): feature_two[:, 0]]
    broadcast_in_dim x0 -> x1, local copies, waits for them, and re-layouts: none -> 0.8 us  [shards(): coreset_index[:, None]]
where the time goes in v2:
time: 65.8 us; the launch traced here: 65.5 us
  Pallas kernels  57.4 us (87%)
  local copies, waits for them, and re-layouts  8.05 us (12%)
    pallas_call x1, Pallas kernels, shards(): pl.pallas_call(roll_map, out_shape=jax.ShapeDtypeStruct((height, width),...  57.4 us
    unnamed x13, local copies, waits for them, and re-layouts  7.25 us

profile of v2, /device:TPU:0, one launch (start us, length us, event | category | flops | bytes accessed | tf_op | source)
XLA Modules:
  0.0 65.5 jit_solution(853050915618760234)
XLA Ops:
  0.0 0.8 %copy.8.index = s32[256,1]{1,0:T(8,128)S(1)} copy(s32[256,1]{0,1:T(1,128)} %bitcast.3) | data formatting | bytes 2048 | tf_op jit(solution)/shard_map/broadcast_in_dim | solution.py:301
  0.8 0.0 copy-start
  0.8 1.4 %copy-done = bf16[8,192,512]{2,1,0:T(8,128)(2,1)S(1)} copy-done((bf16[8,192,512]{2,1,0:T(8,128)(2,1)S(1)}, bf16[8,192,512]{2,1,0:T(8,128)(2,1)}, u32[]{:S(2)}) %copy-start) | copy-done | bytes 1572888
  2.2 0.0 copy-start.1
  2.2 1.2 %copy-done.1 = bf16[512,1024]{1,0:T(8,128)(2,1)S(1)} copy-done((bf16[512,1024]{1,0:T(8,128)(2,1)S(1)}, bf16[512,1024]{1,0:T(8,128)(2,1)}, u32[]{:S(2)}) %copy-start.1) | copy-done | bytes 1048600
  3.5 0.0 copy-start.2
  3.5 1.2 %copy-done.2 = bf16[320,1536]{1,0:T(8,128)(2,1)S(1)} copy-done((bf16[320,1536]{1,0:T(8,128)(2,1)S(1)}, bf16[320,1536]{1,0:T(8,128)(2,1)}, u32[]{:S(2)}) %copy-start.2) | copy-done | bytes 983064
  4.7 0.0 copy-start.3
  4.7 1.1 %copy-done.3 = bf16[4,96,1024]{2,1,0:T(8,128)(2,1)S(1)} copy-done((bf16[4,96,1024]{2,1,0:T(8,128)(2,1)S(1)}, bf16[4,96,1024]{2,1,0:T(8,128)(2,1)}, u32[]{:S(2)}) %copy-start.3) | copy-done | bytes 786456
  5.8 0.0 copy-start.4
  5.8 1.0 %copy-done.4 = bf16[4,96,512]{2,1,0:T(8,128)(2,1)S(1)} copy-done((bf16[4,96,512]{2,1,0:T(8,128)(2,1)S(1)}, bf16[4,96,512]{2,1,0:T(8,128)(2,1)}, u32[]{:S(2)}) %copy-start.4) | copy-done | bytes 393240
  6.8 0.0 copy-start.5
  6.8 0.7 %copy-done.5 = f32[1024]{0:T(1024)S(1)} copy-done((f32[1024]{0:T(1024)S(1)}, f32[1024]{0:T(1024)}, u32[]{:S(2)}) %copy-start.5) | copy-done | bytes 4120
  7.5 57.4 %shard_map.73 = f32[8,192]{1,0:T(8,128)S(1)} custom-call(bf16[8,192,512]{2,1,0:T(8,128)(2,1)S(1)} %copy-done, bf16[4,96,512]{2,1,0:T(8,128)(2,1)S(1)} %copy-done.4, bf16[4,96,1024]{2,1,0:T(8,128)(2,1)S(1)} %copy-done.3, bf16[512,1024]{1,0:T(8,128)(2,1)S(1)} %copy-done.1, f32[1,1024]{1,0:T(1,128)S(1)} %bitcast.2, bf16[320,1536]{1,0:T(8,128)(2,1)S(1)} %copy-done.2, ...), custom_call_target="tpu_custom_call" | custom-call | tf_op jit(solution)/shard_map/pallas_call | solution.py:280
  64.9 0.6 copy.10
Async XLA Ops:
  0.8 1.4 %copy-start = (bf16[8,192,512]{2,1,0:T(8,128)(2,1)S(1)}, bf16[8,192,512]{2,1,0:T(8,128)(2,1)}, u32[]{:S(2)}) copy-start(bf16[8,192,512]{2,1,0:T(8,128)(2,1)} %feature.1) | copy-start | bytes 4718596
  2.2 1.2 %copy-start.1 = (bf16[512,1024]{1,0:T(8,128)(2,1)S(1)}, bf16[512,1024]{1,0:T(8,128)(2,1)}, u32[]{:S(2)}) copy-start(bf16[512,1024]{1,0:T(8,128)(2,1)} %weight.1) | copy-start | bytes 3145732
  3.5 1.2 %copy-start.2 = (bf16[320,1536]{1,0:T(8,128)(2,1)S(1)}, bf16[320,1536]{1,0:T(8,128)(2,1)}, u32[]{:S(2)}) copy-start(bf16[320,1536]{1,0:T(8,128)(2,1)} %bank_rows.1) | copy-start | bytes 2949124
  4.7 1.1 %copy-start.3 = (bf16[4,96,1024]{2,1,0:T(8,128)(2,1)S(1)}, bf16[4,96,1024]{2,1,0:T(8,128)(2,1)}, u32[]{:S(2)}) copy-start(bf16[4,96,1024]{2,1,0:T(8,128)(2,1)} %skip.1) | copy-start | bytes 2359300
  5.8 1.0 %copy-start.4 = (bf16[4,96,512]{2,1,0:T(8,128)(2,1)S(1)}, bf16[4,96,512]{2,1,0:T(8,128)(2,1)}, u32[]{:S(2)}) copy-start(bf16[4,96,512]{2,1,0:T(8,128)(2,1)} %inner.1) | copy-start | bytes 1179652
  6.8 0.7 %copy-start.5 = (f32[1024]{0:T(1024)S(1)}, f32[1024]{0:T(1024)}, u32[]{:S(2)}) copy-start(f32[1024]{0:T(1024)} %param.11) | copy-start | bytes 12292

commit v3 on v2

--- a/solution.py
+++ b/solution.py
@@ -47,8 +47,13 @@
     return pltpu.make_async_remote_copy(src, dst, s, r, device_id=device, device_id_type=MESH)
 
 
-def roll_map(feature, inner, skip, weight, bias, bank_rows, index, out,
-             layer, pack, cores, f_halo, l_halo, packs, pooled, patches, sizes, bests, scores, tiles,
+def halves(x):
+    high = x.astype(BF16)
+    return [high, (x - high.astype(F32)).astype(BF16)]
+
+
+def roll_map(feature_in, inner_in, skip_in, weight_in, bias, bank_in, index, out,
+             feature, inner, skip, weight, bank_rows, load, layer, pack, cores, f_halo, l_halo, packs, pooled, patches, sizes, bests, scores, tiles,
              z_send, z_recv, y_send, y_recv, c_send, c_recv, h_send, h_recv, t_send, t_recv):
     circ, span, bank = (lax.axis_index(a) for a in ("circ", "len", "bank"))
     n_len, n_bank = lax.axis_size("len"), lax.axis_size("bank")
@@ -57,6 +62,10 @@
     mate = (span // 2) * 2 + 1 - lax.rem(span, 2)
     z_peers = [(circ, span, lax.rem(bank + d, n_bank)) for d in range(1, n_bank)]
     y_peer, c_peer = (circ, across, bank), (circ, mate, bank)
+    pairs = [(bank_in, bank_rows), (inner_in, inner), (weight_in, weight), (skip_in, skip), (feature_in, feature)]
+    loads = [pltpu.make_async_copy(src, dst, load.at[n]) for n, (src, dst) in enumerate(pairs)]
+    for copy in loads:
+        copy.start()
     meet([up, down] + sides + corners + z_peers + [y_peer, c_peer])
     height, width, c2 = feature.shape
     deep, wide, c3 = skip.shape
@@ -67,13 +76,26 @@
 
     halo = [
         (layer.at[deep - 1], l_halo.at[1], down), (layer.at[0], l_halo.at[2], up),
-        (feature.at[height - 1], f_halo.at[0], down), (feature.at[0], f_halo.at[1], up),
+        (feature_in.at[height - 1], f_halo.at[0], down), (feature_in.at[0], f_halo.at[1], up),
         (layer.at[deep - 2], l_halo.at[0], down), (layer.at[1], l_halo.at[3], up),
         (pack, packs.at[3], sides[0]), (pack, packs.at[0], sides[1]),
         (pack, packs.at[5], corners[0]), (pack, packs.at[4], corners[1]),
         (pack, packs.at[2], corners[2]), (pack, packs.at[1], corners[3]),
     ]
     h = [send(s, d, h_send.at[i], h_recv.at[i], to) for i, (s, d, to) in enumerate(halo)]
+
+    h[2].start()
+    h[3].start()
+    chosen = index[...] == lax.broadcasted_iota(jnp.int32, (bank_rows.shape[0], cores.shape[1]), 0)
+    loads[0].wait()
+    cores[0] = lax.dot_general(jnp.where(chosen, 1.0, 0.0).astype(BF16), bank_rows[...],
+                               (((0,), (0,)), ((), ())), preferred_element_type=F32).astype(BF16)
+    z = [send(cores.at[0, rows(span)], cores.at[d + 1, rows(span)], z_send.at[d], z_recv.at[d], z_peers[d])
+         for d in range(n_bank - 1)]
+    for copy in z:
+        copy.start()
+    for copy in loads[1:]:
+        copy.wait()
 
     sixteen = lax.broadcasted_iota(jnp.int32, (16, c3), 0)
     packed = jnp.zeros((16, c3), F32)
@@ -90,8 +112,6 @@
             h[0].start()
         if r == 0:
             h[1].start()
-            h[2].start()
-            h[3].start()
     pack[:, c2:] = packed.astype(BF16)
     sixteen = lax.broadcasted_iota(jnp.int32, (16, c2), 0)
     packed = jnp.zeros((16, c2), F32)
@@ -102,14 +122,6 @@
     for copy in h[6:]:
         copy.start()
 
-    chosen = index[...] == lax.broadcasted_iota(jnp.int32, (cores.shape[1], bank_rows.shape[0]), 1)
-    cores[0] = jnp.dot(jnp.where(chosen, 1.0, 0.0).astype(BF16), bank_rows[...],
-                       preferred_element_type=F32).astype(BF16)
-    z = [send(cores.at[0, rows(span)], cores.at[d + 1, rows(span)], z_send.at[d], z_recv.at[d], z_peers[d])
-         for d in range(n_bank - 1)]
-    for copy in z:
-        copy.start()
-
     lead = jnp.where(at_start, 0.0, 1.0)
     trail = jnp.where(at_end, 0.0, 1.0)
     for copy in h[6:]:
@@ -141,10 +153,10 @@
     def pool_three(k):
         s = l_row(k - 1) + l_row(k) + l_row(k + 1)
         e = [[sum(l_edge(side, k + t, column) for t in (-1, 0, 1)) for column in (0, 1)] for side in (0, 1)]
-        q = ((s + shift_rows(s, 1, e[0][1]) + shift_rows(s, -1, e[1][0])) / 9.0).astype(BF16)
+        q = ((s + shift_rows(s, 1, e[0][1]) + shift_rows(s, -1, e[1][0])) * (1.0 / 9.0)).astype(BF16)
         pooled[k + 1] = q
-        first = ((e[0][0] + e[0][1] + s[0:1]) / 9.0).astype(BF16).astype(F32)
-        last = ((s[wide - 1:wide] + e[1][0] + e[1][1]) / 9.0).astype(BF16).astype(F32)
+        first = ((e[0][0] + e[0][1] + s[0:1]) * (1.0 / 9.0)).astype(BF16).astype(F32)
+        last = ((s[wide - 1:wide] + e[1][0] + e[1][1]) * (1.0 / 9.0)).astype(BF16).astype(F32)
         qf = q.astype(F32)
         q_lead[k + 1] = jnp.where(at_start, qf[0:1], first)
         q_trail[k + 1] = jnp.where(at_end, qf[wide - 1:wide], last)
@@ -156,27 +168,28 @@
     stretch = jnp.where(j == k, 0.75, jnp.where(j == near, 0.25, 0.0)).astype(F32)
     main_w = (0.75 * stretch).astype(BF16)
     side_w = (0.25 * stretch).astype(BF16)
-    row_id = lax.broadcasted_iota(jnp.int32, (width, c3), 0)
-    ones = jnp.ones((8, 128), F32)
+    row_id = lax.broadcasted_iota(jnp.int32, (8, c3), 0)
+    ones = jnp.ones((8, 256), BF16)
 
     def make_patch(r):
         s = f_row(r - 1) + f_row(r) + f_row(r + 1)
         e = [sum(f_edge(side, r + t) for t in (-1, 0, 1)) for side in (0, 1)]
-        two = ((s + shift_rows(s, 1, e[0]) + shift_rows(s, -1, e[1])) / 9.0).astype(BF16)
+        two = ((s + shift_rows(s, 1, e[0]) + shift_rows(s, -1, e[1])) * (1.0 / 9.0)).astype(BF16)
         a = r // 2 + 1
         b = a + (1 if r % 2 else -1)
         u = jnp.dot(main_w, pooled[a], preferred_element_type=F32)
         u = u + jnp.dot(side_w, pooled[b], preferred_element_type=F32)
         begin = 0.25 * (0.75 * q_lead[a] + 0.25 * q_lead[b])
         end = 0.25 * (0.75 * q_trail[a] + 0.25 * q_trail[b])
-        u = u + jnp.where(row_id == 0, begin, 0.0) + jnp.where(row_id == width - 1, end, 0.0)
+        u = jnp.concatenate([u[:8] + jnp.where(row_id == 0, begin, 0.0), u[8:width - 8],
+                             u[width - 8:] + jnp.where(row_id == 7, end, 0.0)], axis=0)
         patch = jnp.concatenate([two, u.astype(BF16)], axis=1)
         patches[r] = patch
         wide_patch = patch.astype(F32)
         square = wide_patch * wide_patch
         folded = sum(square[:, t:t + 128] for t in range(0, c2 + c3, 128))
-        sizes[r] = lax.dot_general(ones, folded, (((1,), (1,)), ((), ())),
-                                   precision=lax.Precision.HIGHEST, preferred_element_type=F32)
+        sizes[r] = lax.dot_general(ones, jnp.concatenate(halves(folded), axis=1), (((1,), (1,)), ((), ())),
+                                   preferred_element_type=F32)
 
     for k in range(1, deep - 1):
         pool_three(k)
@@ -254,17 +267,22 @@
         return taps(j - i + offset)
 
     def dot(a, b):
-        return jnp.dot(a, b, precision=lax.Precision.HIGHEST, preferred_element_type=F32)
-
-    vertical = band((height, 3 * height), -height)
-    bands = [band((width, width), offset) for offset in (0, width, -width)]
+        a = halves(a)
+        both = jnp.dot(jnp.concatenate(a, axis=0), b[0], preferred_element_type=F32)
+        return both[:height] + both[height:] + jnp.dot(a[0], b[1], preferred_element_type=F32)
+
+    def fall(above, here, below):
+        x = jnp.concatenate([above, here, below], axis=0)
+        return sum(BLUR_TAPS[n] * x[height - 2 + n:2 * height - 2 + n] for n in range(5))
+
+    bands = [halves(band((width, width), offset)) for offset in (0, width, -width)]
     for copy in z + y + c + h:
         copy.wait_send()
     for copy in t:
         copy.wait_recv()
-    middle = dot(vertical, jnp.concatenate([tiles[0], found, tiles[1]], axis=0))
-    left = dot(vertical, jnp.concatenate([tiles[3], tiles[2], tiles[4]], axis=0)) * lead
-    right = dot(vertical, jnp.concatenate([tiles[6], tiles[5], tiles[7]], axis=0)) * trail
+    middle = fall(tiles[0], found, tiles[1])
+    left = fall(tiles[3], tiles[2], tiles[4]) * lead
+    right = fall(tiles[6], tiles[5], tiles[7]) * trail
     out[...] = dot(middle, bands[0]) + dot(left, bands[1]) + dot(right, bands[2])
     for copy in t:
         copy.wait_send()
@@ -276,13 +294,16 @@
     n_bank = lax.axis_size("bank")
     cores = coreset_index.shape[0]
     vm = pl.BlockSpec(memory_space=VMEM)
+    hbm = pl.BlockSpec(memory_space=pl.ANY)
     dma = pltpu.SemaphoreType.DMA
     return pl.pallas_call(
         roll_map,
         out_shape=jax.ShapeDtypeStruct((height, width), F32),
-        in_specs=[vm] * 7,
+        in_specs=[hbm] * 4 + [vm, hbm, vm],
         out_specs=vm,
         scratch_shapes=[
+            VMEM(feature_two.shape, BF16), VMEM(inner_three.shape, BF16), VMEM(skip_three.shape, BF16),
+            VMEM(out_weight.shape, BF16), VMEM(bank_rows.shape, BF16), dma((5,)),
             VMEM((deep, wide, c3), BF16),
             VMEM((16, c2 + c3), BF16),
             VMEM((n_bank, cores, c2 + c3), BF16),
@@ -297,8 +318,8 @@
             VMEM((8, height, width), F32),
         ] + [dma((n_bank - 1,))] * 4 + [dma((2 * (n_bank - 1),))] * 2 + [dma((12,))] * 2 + [dma((8,))] * 2,
         compiler_params=pltpu.CompilerParams(
-            collective_id=0, has_side_effects=True, vmem_limit_bytes=48 * 2**20),
-    )(feature_two, inner_three, skip_three, out_weight, out_bias[None, :], bank_rows, coreset_index[:, None])
+            collective_id=0, has_side_effects=True, vmem_limit_bytes=60 * 2**20),
+    )(feature_two, inner_three, skip_three, out_weight, out_bias[None, :], bank_rows, coreset_index[None, :])
 
 
 def solution(mesh):

time: 65.8 us -> 64.3 us (0.977)
  local copies, waits for them, and re-layouts: 8.05 us -> 1.3 us
  Pallas kernels: 57.4 us -> 62.7 us
    unnamed x13 -> x1, local copies, waits for them, and re-layouts: 7.25 us -> 1.3 us
    pallas_call x1, Pallas kernels: 57.4 us -> 62.7 us  [shards(): pl.pallas_call(roll_map, out_shape=jax.ShapeDtypeStruct((height, width),...]
    broadcast_in_dim x1 -> x0, local copies, waits for them, and re-layouts: 0.8 us -> none  [shards(): coreset_index[:, None]]
where the time goes in v3:
time: 64.3 us; the launch traced here: 64 us
  Pallas kernels  62.7 us (98%)
  local copies, waits for them, and re-layouts  1.3 us (2%)
    pallas_call x1, Pallas kernels, shards(): pl.pallas_call(roll_map, out_shape=jax.ShapeDtypeStruct((height, width),...  62.7 us
    unnamed x1, local copies, waits for them, and re-layouts  1.3 us

profile of v3, /device:TPU:0, one launch (start us, length us, event | category | flops | bytes accessed | tf_op | source)
XLA Modules:
  0.0 64.0 jit_solution(4415293302293001433)
XLA Ops:
  0.0 62.7 %shard_map.73 = f32[8,192]{1,0:T(8,128)} custom-call(bf16[8,192,512]{2,1,0:T(8,128)(2,1)} %feature_in.1, bf16[4,96,512]{2,1,0:T(8,128)(2,1)} %inner_in.1, bf16[4,96,1024]{2,1,0:T(8,128)(2,1)} %skip_in.1, bf16[512,1024]{1,0:T(8,128)(2,1)} %weight_in.1, f32[1,1024]{1,0:T(1,128)} %bitcast.2, bf16[320,1536]{1,0:T(8,128)(2,1)} %bank_in.1, s32[1,256]{1,0:T(1,128)} %bitcast.3), custom_call_target="tpu_custom_call" | custom-call | tf_op jit(solution)/shard_map/pallas_call | solution.py:299
  62.7 1.3 %copy.9 = f32[8,192]{1,0:T(8,128)} copy(f32[8,192]{1,0:T(8,128)} %shard_map.73) | data formatting | bytes 12288

commit v4 on v3

--- a/solution.py
+++ b/solution.py
@@ -217,32 +217,39 @@
         e = n_bank - 1 + d
         c.append(send(here, here, c_send.at[e], c_recv.at[e], c_peer))
         c[-1].start()
-    for copy in c:
-        copy.wait_recv()
-
     norms = []
-    for part in range(n_bank):
-        wide_core = cores[part].astype(F32)
-        norms.append(jnp.sum(wide_core * wide_core, axis=1, keepdims=True))
-
-    def score_row(r, carry):
+
+    def score_row(r, parts):
         patch = patches[r]
         best = None
-        for part in range(n_bank):
+        for part in parts:
             product = lax.dot_general(cores[part], patch, (((1,), (1,)), ((), ())), preferred_element_type=F32)
             low = jnp.min(norms[part] - 2.0 * product, axis=0, keepdims=True)
             best = low if best is None else jnp.minimum(best, low)
-        bests[r] = jnp.broadcast_to(best, bests.shape[1:])
-        return carry
-
-    lax.fori_loop(1, height - 1, score_row, 0)
+        best = jnp.broadcast_to(best, bests.shape[1:])
+        bests[r] = best if parts[0] == 0 else jnp.minimum(bests[r], best)
+
+    def score_rows(first, last, step, parts):
+        def body(n, carry):
+            score_row(first + step * n, parts)
+            return carry
+
+        lax.fori_loop(0, last, body, 0)
+
+    for part in range(n_bank):
+        if part:
+            c[part - 1].wait_recv()
+            c[n_bank - 2 + part].wait_recv()
+        wide_core = cores[part].astype(F32)
+        norms.append(jnp.sum(wide_core * wide_core, axis=1, keepdims=True))
+        score_rows(1, height - 2, 1, [part])
     for copy in h[2:6]:
         copy.wait_recv()
     pool_three(-1)
     pool_three(deep)
     make_patch(0)
     make_patch(height - 1)
-    lax.fori_loop(0, 2, lambda n, carry: score_row(n * (height - 1), carry), 0)
+    score_rows(0, 2, height - 1, list(range(n_bank)))
 
     eight = lax.broadcasted_iota(jnp.int32, (height, width), 0)
     found = jnp.zeros((height, width), F32)

time: 64.3 us -> 67.8 us (1.054)
  Pallas kernels: 62.7 us -> 66.2 us
    pallas_call x1, Pallas kernels: 62.7 us -> 66.2 us  [shards(): pl.pallas_call(roll_map, out_shape=jax.ShapeDtypeStruct((height, width),...]
where the time goes in v4:
time: 67.8 us; the launch traced here: 67.6 us
  Pallas kernels  66.2 us (98%)
  local copies, waits for them, and re-layouts  1.3 us (2%)
    pallas_call x1, Pallas kernels, shards(): pl.pallas_call(roll_map, out_shape=jax.ShapeDtypeStruct((height, width),...  66.2 us

profile of v4, /device:TPU:0, one launch (start us, length us, event | category | flops | bytes accessed | tf_op | source)
XLA Modules:
  0.0 67.6 jit_solution(10957659574521249747)
XLA Ops:
  0.0 66.2 %shard_map.73 = f32[8,192]{1,0:T(8,128)} custom-call(bf16[8,192,512]{2,1,0:T(8,128)(2,1)} %feature_in.1, bf16[4,96,512]{2,1,0:T(8,128)(2,1)} %inner_in.1, bf16[4,96,1024]{2,1,0:T(8,128)(2,1)} %skip_in.1, bf16[512,1024]{1,0:T(8,128)(2,1)} %weight_in.1, f32[1,1024]{1,0:T(1,128)} %bitcast.2, bf16[320,1536]{1,0:T(8,128)(2,1)} %bank_in.1, s32[1,256]{1,0:T(1,128)} %bitcast.3), custom_call_target="tpu_custom_call" | custom-call | tf_op jit(solution)/shard_map/pallas_call | solution.py:306
  66.3 1.3 %copy.9 = f32[8,192]{1,0:T(8,128)} copy(f32[8,192]{1,0:T(8,128)} %shard_map.73) | data formatting | bytes 12288
